TPU v7x, 256 devices: a whole 4x4x8 slice. The times are simulated.
256 devices in a mesh: blk: 32 (over x, z), chan: 8 (over y, core).
Axes of the slice: x: 4, y: 4, z: 8, core: 2. Of those that a mesh axis runs over, the one named last changes fastest.
Arguments:
- sky_map: bfloat16 [1792, 128, 2048], P('blk', 'chan'), may hold values from -6 to 6
- cycle_weight: float32 [1792], P('blk'), may hold values from 0.5 to 2
- legendre: bfloat16 [256, 1536, 1792], P('blk', 'chan'), may hold values from -0.125 to 0.125
- kl_filter: bfloat16 [1536, 128, 128], P('chan'), may hold values from -0.5 to 0.5
Outputs:
- filtered_map: bfloat16 [1792, 128, 2048], P('blk', 'chan')
All inputs are finite; a program needn't handle non-finite values.
Results may differ from a plain program's by a relative error of at most 0.02.
Values may be sent and summed in bfloat16 or wider, within the bound.
A program may use at most 128 MiB of HBM per device.

v0:
```python
import math

import jax
import jax.numpy as jnp
from jax import lax
from jax.sharding import PartitionSpec as P


def transform_table(pixel_count, mode_count):
    pixel_index = jnp.arange(pixel_count, dtype=jnp.int32)
    mode_index = jnp.arange(mode_count, dtype=jnp.int32)
    phase_index = pixel_index[:, None] * mode_index[None, :] % pixel_count
    angles = phase_index.astype(jnp.float32) * (2.0 * math.pi / pixel_count)
    return jnp.concatenate([jnp.cos(angles), -jnp.sin(angles)], axis=1).astype(jnp.bfloat16)


def shards(sky_map, cycle_weight, legendre, kl_filter):
    rows_here, chans_here, pixel_count = sky_map.shape
    slots_here, bands_here, cycle_count = legendre.shape
    mode_count = slots_here * lax.axis_size("blk")
    fourier_table = transform_table(pixel_count, mode_count)
    flat_map = sky_map.reshape(rows_here * chans_here, pixel_count)
    spectra = jnp.dot(flat_map, fourier_table, preferred_element_type=jnp.float32)
    scaled = spectra.reshape(rows_here, chans_here, 2 * mode_count) * (
        cycle_weight[:, None, None] / math.sqrt(pixel_count)
    )
    spectra = scaled.astype(jnp.bfloat16).reshape(rows_here, chans_here, 2, mode_count)
    cycle_spectra = lax.all_to_all(spectra, "blk", split_axis=3, concat_axis=0, tiled=True)
    first_mode = lax.axis_index("blk") * slots_here
    first_band = lax.axis_index("chan") * bands_here
    mode_ids = first_mode + jnp.arange(slots_here, dtype=jnp.int32)
    degree_ids = first_band + jnp.arange(bands_here, dtype=jnp.int32)
    keep_mask = degree_ids[None, :] >= mode_ids[:, None]
    masked = jnp.where(keep_mask[:, :, None], legendre, jnp.zeros_like(legendre))
    coeffs = jnp.einsum(
        "mlr,rcpm->mlpc",
        masked,
        lax.all_gather(cycle_spectra, "chan", axis=1, tiled=True),
        preferred_element_type=jnp.float32,
    )
    coeffs = coeffs.astype(jnp.bfloat16)
    filtered = jnp.einsum(
        "lcd,mlpd->mlpc", kl_filter, coeffs, preferred_element_type=jnp.float32
    ).astype(jnp.bfloat16)
    synth_field = lax.psum_scatter(
        jnp.einsum("mlr,mlpc->crpm", masked, filtered, preferred_element_type=jnp.float32).astype(
            jnp.bfloat16
        ),
        "chan",
        scatter_dimension=0,
        tiled=True,
    )
    cycle_field = lax.all_to_all(synth_field, "blk", split_axis=1, concat_axis=3, tiled=True)
    cycle_field = cycle_field.reshape(chans_here, rows_here, 2 * mode_count)
    output = jnp.einsum(
        "crk,pk->rcp", cycle_field, fourier_table, preferred_element_type=jnp.float32
    )
    return (output / math.sqrt(pixel_count)).astype(jnp.bfloat16)


def solution(mesh):
    in_specs = (P("blk", "chan", None), P("blk"), P("blk", "chan", None), P("chan", None, None))
    out_specs = P("blk", "chan", None)
    return jax.shard_map(shards, mesh=mesh, in_specs=in_specs, out_specs=out_specs, check_vma=False)
```

profile of v0, /device:TPU:32, one launch (start us, length us, event | category | flops | bytes accessed | tf_op | source)
XLA Modules:
  0.0 312.5 jit_solution(14384071588572710647)
XLA Ops:
  6.5 8.5 %negate_convert_fusion = (bf16[2048,256]{1,0:T(8,128)(2,1)S(1)}, bf16[2048,256]{1,0:T(8,128)(2,1)S(1)}) fusion(), kind=kLoop, calls=%fused_computation.20 | loop fusion | flops 8912896 | bytes 2097152 | tf_op jit(solution)/shard_map/convert.1
  15.1 0.0 copy-done.3
  15.1 0.0 copy-start
  15.1 0.0 copy-start.2
  15.1 1.0 copy-done
  16.1 0.4 copy-done.2
  16.5 5.6 %convolution_bitcast_fusion = f32[896,512]{0,1:T(8,128)} fusion(bf16[896,2048]{1,0:T(8,128)(2,1)} %bitcast.59, bf16[2048,256]{1,0:T(8,128)(2,1)S(1)} %get-tuple-element.5, bf16[2048,256]{1,0:T(8,128)(2,1)S(1)} %get-tuple-element.6), kind=kOutput, calls=%fused_computation.27 | convolution fusion | flops 1883242496 | bytes 7602176 | tf_op jit(solution)/shard_map/dot_general | solution.py:23
  22.1 1.8 copy.43
  24.0 2.4 reshape.50
  26.3 1.7 fusion.18
  28.0 3.4 %copy.45 = bf16[56,16,2,256]{0,1,2,3:T(8,128)(2,1)S(1)} copy(bf16[56,16,2,256]{3,1,2,0:T(8,128)(2,1)S(1)} %fusion.18) | data formatting | bytes 1835008 | tf_op jit(solution)/shard_map/convert_element_type | solution.py:27
  31.4 3.7 %reshape.56 = bf16[32,2,7168]{2,1,0:T(2,128)(2,1)S(1)} reshape(bf16[256,2,16,56]{3,2,1,0:T(8,128)(2,1)S(1)} %bitcast.56) | data formatting | bytes 1835008
  35.1 36.9 %all_to_all.33 = bf16[32,2,7168]{2,1,0:T(2,128)(2,1)} all-to-all(bf16[32,2,7168]{2,1,0:T(2,128)(2,1)S(1)} %reshape.56), channel_id=1, replica_groups=mesh['blk'=32,'chan'=8] {'blk'}, dimensions={0} | all-to-all | bytes 1835008 | tf_op jit(solution)/shard_map/all_to_all | solution.py:28
  72.0 5.7 %reshape.57 = bf16[256,2,16,56]{3,2,1,0:T(8,128)(2,1)S(1)} reshape(bf16[32,2,7168]{2,1,0:T(2,128)(2,1)} %all_to_all.33) | data formatting | bytes 1835008
  77.7 2.7 copy.59
  80.4 4.7 %reshape.55 = bf16[1792,16,2,8]{0,1,2,3:T(8,128)(2,1)} reshape(bf16[32,56,16,2,8]{1,0,2,3,4:T(8,128)(2,1)} %copy.59) | data formatting | bytes 1835008 | tf_op jit(solution)/shard_map/all_to_all | solution.py:28
  85.1 0.0 all-gather.2.cloned.1.call-update
  85.2 0.3 reduce-scatter.2.cloned.1.call-start
  85.5 0.1 broadcast_compare_fusion
  85.5 44.1 %all-gather.2.cloned.1.call-done = bf16[1792,128,2,8]{0,1,2,3:T(8,128)(2,1)} async-done(((bf16[1792,16,2,8]{0,1,2,3:T(8,128)(2,1)}), bf16[1792,128,2,8]{0,1,2,3:T(8,128)(2,1)}) %all-gather.2.cloned.1.call-update) | async-done | bytes 7340048 | tf_op jit(solution)/shard_map/all_gather | solution.py:38
  129.7 7.2 %fusion.25 = bf16[8,192,2,128]{3,1,2,0:T(8,128)(2,1)S(1)} fusion(bf16[1792,128,2,8]{0,1,2,3:T(8,128)(2,1)} %all-gather.2.cloned.1.call-done, bf16[8,192,1792]{2,1,0:T(8,128)(2,1)} %param.6, pred[8,192]{1,0:T(8,128)(4,1)S(1)} %broadcast_compare_fusion), kind=kOutput, calls=%fused_computation.30 | convolution fusion | flops 1412431872 | bytes 13633024 | tf_op jit(solution)/shard_map/mlr,rcpm->mlpc/dot_general | solution.py:35
  136.9 6.1 %fusion.28 = bf16[8,192,2,128]{3,0,2,1:T(8,128)(2,1)S(1)} fusion(bf16[192,128,128]{2,1,0:T(8,128)(2,1)} %param.7, bf16[8,192,2,128]{3,1,2,0:T(8,128)(2,1)S(1)} %fusion.25), kind=kOutput, calls=%fused_computation.31 | convolution fusion | flops 101056512 | bytes 7864320 | tf_op jit(solution)/shard_map/lcd,mlpd->mlpc/dot_general | solution.py:42
  143.0 7.7 %convert_bitcast_fusion = bf16[128,1792,2,8]{1,0,2,3:T(8,128)(2,1)} fusion(bf16[8,192,1792]{2,1,0:T(8,128)(2,1)} %param.6, pred[8,192]{1,0:T(8,128)(4,1)S(1)} %broadcast_compare_fusion, bf16[8,192,2,128]{3,0,2,1:T(8,128)(2,1)S(1)} %fusion.28), kind=kOutput, calls=%fused_computation.1 | convolution fusion | flops 1415708672 | bytes 13633024 | tf_op jit(solution)/shard_map/mlr,mlpc->crpm/dot_general | solution.py:46
  150.7 0.0 reduce-scatter.2.cloned.1.call-update
  150.8 50.3 %reduce-scatter.2.cloned.1.call-done = bf16[16,1792,2,8]{1,0,2,3:T(8,128)(2,1)} async-done(((bf16[128,1792,2,8]{1,0,2,3:T(8,128)(2,1)}), bf16[16,1792,2,8]{1,0,2,3:T(8,128)(2,1)}) %reduce-scatter.2.cloned.1.call-update) | async-done | bytes 917520 | tf_op jit(solution)/shard_map/reduce_scatter | solution.py:45
  201.1 15.2 %copy.51 = bf16[16,1792,2,8]{0,2,3,1:T(2,128)(2,1)} copy(bf16[16,1792,2,8]{1,0,2,3:T(8,128)(2,1)} %reduce-scatter.2.cloned.1.call-done) | data formatting | bytes 1835008 | tf_op jit(solution)/shard_map/reduce_scatter | solution.py:45
  216.3 20.5 %reshape.58 = bf16[32,2,7168]{2,1,0:T(2,128)(2,1)S(1)} reshape(bf16[1792,8,2,16]{3,2,1,0:T(2,128)(2,1)} %bitcast.54) | data formatting | bytes 1835008
  236.8 35.1 %all_to_all.34 = bf16[32,2,7168]{2,1,0:T(2,128)(2,1)S(1)} all-to-all(bf16[32,2,7168]{2,1,0:T(2,128)(2,1)S(1)} %reshape.58), channel_id=1, replica_groups=mesh['blk'=32,'chan'=8] {'blk'}, dimensions={0} | all-to-all | bytes 1835008 | tf_op jit(solution)/shard_map/all_to_all | solution.py:53
  272.0 6.4 %reshape.59 = bf16[1792,8,2,16]{3,2,1,0:T(2,128)(2,1)} reshape(bf16[32,2,7168]{2,1,0:T(2,128)(2,1)S(1)} %all_to_all.34) | data formatting | bytes 1835008
  278.3 20.1 %copy.52 = bf16[16,32,56,2,8]{2,4,1,3,0:T(8,128)(2,1)S(1)} copy(bf16[16,32,56,2,8]{0,3,4,2,1:T(2,128)(2,1)} %bitcast.55) | data formatting | bytes 1835008 | tf_op jit(solution)/shard_map/all_to_all | solution.py:53
  298.4 3.4 %fusion.8 = bf16[56,16,2048]{2,0,1:T(8,128)(2,1)S(1)} fusion(bf16[16,56,512]{1,2,0:T(8,128)(2,1)S(1)} %bitcast.58, bf16[2048,256]{1,0:T(8,128)(2,1)S(1)} %copy-done.1, bf16[2048,256]{1,0:T(8,128)(2,1)} %copy-done.2), kind=kOutput, calls=%fused_computation.12 | convolution fusion | flops 1886912512 | bytes 6684672 | tf_op jit(solution)/shard_map/crk,pk->rcp/dot_general | solution.py:55
  301.8 3.8 %copy.54 = bf16[56,16,2048]{2,1,0:T(8,128)(2,1)} copy(bf16[56,16,2048]{2,0,1:T(8,128)(2,1)S(1)} %fusion.8) | data formatting | bytes 7340032 | tf_op jit(solution)/shard_map/convert_element_type | solution.py:58
  (7 shorter events, 0.0 us)
Async XLA Ops:
  6.5 8.6 %copy-start.3 = (f32[56]{0:T(128)S(1)}, f32[56]{0:T(128)}, u32[]{:S(2)}) copy-start(f32[56]{0:T(128)} %param.5) | copy-start | bytes 676
  6.5 123.1 %all-gather.2.cloned.1.call-start = ((), (), s32[]{:S(2)}) async-start(), calls=%async_computation.3 | async-start | bytes 8257536 | tf_op jit(solution)/shard_map/all_gather | solution.py:38
  15.1 1.0 copy-start
  15.1 1.4 copy-start.2
  85.2 115.9 %reduce-scatter.2.cloned.1.call-start = ((), (), s32[]{:S(2)}) async-start(), calls=%async_computation.4 | async-start | bytes 8257536 | tf_op jit(solution)/shard_map/reduce_scatter | solution.py:45
  278.3 20.1 %copy-start.1 = (bf16[2048,256]{1,0:T(8,128)(2,1)S(1)}, bf16[2048,256]{1,0:T(8,128)(2,1)}, u32[]{:S(2)}) copy-start(bf16[2048,256]{1,0:T(8,128)(2,1)} %copy-done) | copy-start | bytes 3145732
Sparse Core Ops, SparseCore 0:
  85.3 44.3 all-gather.1
  150.9 50.1 reduce-scatter.1
where the time goes:
time: 315 us; the launch traced here: 312 us
  waiting for transfers between devices  94.5 us (30%)
  local copies, waits for them, and re-layouts  91.8 us (29%)
  blocking collectives  72.1 us (23%)
  matrix products  30 us (10%)
  between operations  13.5 us (4%)
  other arithmetic  10.3 us (3%)
    reduce_scatter x1, waiting for transfers between devices, shards(): lax.psum_scatter(jnp.einsum('mlr,mlpc->crpm', masked, filtered, preferred...  50.3 us
    all_gather x1, waiting for transfers between devices, shards(): lax.all_gather(cycle_spectra, 'chan', axis=1, tiled=True)  44.1 us
    unnamed x12, local copies, waits for them, and re-layouts  37.6 us
    all_to_all x1, blocking collectives, shards(): lax.all_to_all(spectra, 'blk', split_axis=3, concat_axis=0, tiled=True)  36.9 us
    all_to_all x1, blocking collectives, shards(): lax.all_to_all(synth_field, 'blk', split_axis=1, concat_axis=3, tiled=True)  35.1 us
    all_to_all x1, local copies, waits for them, and re-layouts, shards(): lax.all_to_all(synth_field, 'blk', split_axis=1, concat_axis=3, tiled=True)  20.1 us
    reduce_scatter x1, local copies, waits for them, and re-layouts, shards(): lax.psum_scatter(jnp.einsum('mlr,mlpc->crpm', masked, filtered, preferred...  15.2 us
    another operation x1, other arithmetic  8.55 us
  transfers between devices with their start and end apart: 2, of which 2 were waited for; matrix products, arithmetic and copies ran while one was open for 0% of the time, Pallas kernels for 0%

commit v1 on v0

v1 whole, which is shorter than its diff:
```python
import functools
import math

import jax
import jax.numpy as jnp
import numpy as np
from jax import lax
from jax.experimental import pallas as pl
from jax.experimental.pallas import tpu as pltpu
from jax.sharding import PartitionSpec as P

F32, BF16 = jnp.float32, jnp.bfloat16
MESH = pl.DeviceIdType.MESH
NT = (((1,), (1,)), ((), ()))
TN = (((0,), (0,)), ((), ()))
NN = (((1,), (0,)), ((), ()))
VMEM_LIMIT = 60 * 2**20
CHUNKS = 4
GX, GZ, GY = 4, 8, 4
NB = GX * GZ


def fourier_table(pixel_count, mode_count):
    phase = np.arange(pixel_count)[:, None] * np.arange(mode_count)[None, :] % pixel_count
    angles = phase.astype(np.float32) * np.float32(2.0 * math.pi / pixel_count)
    table = np.concatenate([np.cos(angles), -np.sin(angles)], axis=1)
    return table.astype(jnp.bfloat16)


def identity(size):
    rows = lax.broadcasted_iota(jnp.int32, (size, size), 0)
    cols = lax.broadcasted_iota(jnp.int32, (size, size), 1)
    return jnp.where(rows == cols, 1.0, 0.0)


def dot(a, b, dims):
    return lax.dot_general(a, b, dims, preferred_element_type=F32)


def forward_kernel(rows, chans, scale, sky_ref, weight_ref, table_ref, out_ref, spec, turned):
    step, steps = pl.program_id(0), pl.num_programs(0)
    block = sky_ref.shape[0]
    x = dot(sky_ref[...], table_ref[...], NN)
    start = pl.multiple_of(step * block, block)
    for t in range(4):
        spec[t, pl.ds(start, block), :] = x[:, 128 * t : 128 * (t + 1)]

    @pl.when(step == steps - 1)
    def _():
        weight = jnp.sum(identity(rows) * weight_ref[...], axis=1, keepdims=True) * scale
        eye = identity(256).astype(BF16)
        pad = jnp.zeros((64 - rows, 256), F32)
        for c in range(chans):
            quarter = [spec[t, pl.ds(c, rows, stride=chans), :] * weight for t in range(4)]
            real = jnp.concatenate(quarter[:2], axis=1)
            imag = jnp.concatenate(quarter[2:], axis=1)
            both = jnp.concatenate([real, pad, imag, pad], axis=0).astype(BF16)
            turned[pl.ds(c, 256, stride=chans), :] = dot(eye, both, NT)
        out_ref[...] = turned[...].astype(BF16)


def forward(sky, weight, table):
    rows, chans, pixels = sky.shape
    steps = 2
    block = rows * chans // steps
    return pl.pallas_call(
        functools.partial(forward_kernel, rows, chans, 1.0 / math.sqrt(pixels)),
        grid=(steps,),
        out_shape=jax.ShapeDtypeStruct((256 * chans, 128), BF16),
        in_specs=[
            pl.BlockSpec((block, pixels), lambda i: (i, 0)),
            pl.BlockSpec((1, rows), lambda i: (0, 0)),
            pl.BlockSpec((pixels, 512), lambda i: (0, 0)),
        ],
        out_specs=pl.BlockSpec((256 * chans, 128), lambda i: (0, 0)),
        scratch_shapes=[
            pltpu.VMEM((4, rows * chans, 128), F32),
            pltpu.VMEM((256 * chans, 128), F32),
        ],
        compiler_params=pltpu.CompilerParams(vmem_limit_bytes=VMEM_LIMIT),
    )(sky.reshape(rows * chans, pixels), weight.reshape(1, rows), table)


def inverse_kernel(rows, chans, scale, field_ref, table_ref, out_ref, wide, lhs):
    step = pl.program_id(0)
    block = out_ref.shape[0]

    @pl.when(step == 0)
    def _():
        wide[...] = field_ref[...].astype(F32)
        eye = identity(128).astype(BF16)
        for c in range(chans):
            here = wide[pl.ds(c, 256, stride=chans), :].astype(BF16)
            turned = dot(eye, here, NT)
            for h in range(2):
                half = turned[:, 128 * h : 128 * (h + 1)]
                lhs[h, pl.ds(c, rows, stride=chans), :] = half[:rows]
                lhs[2 + h, pl.ds(c, rows, stride=chans), :] = half[64 : 64 + rows]

    start = pl.multiple_of(step * block, block)
    left = jnp.concatenate([lhs[t, pl.ds(start, block), :] for t in range(4)], axis=1).astype(BF16)
    for n in range(0, out_ref.shape[1], 512):
        out_ref[:, n : n + 512] = (dot(left, table_ref[:, n : n + 512], NN) * scale).astype(BF16)


def inverse(field, table, rows, chans):
    pixels = table.shape[1]
    steps = 4
    block = rows * chans // steps
    out = pl.pallas_call(
        functools.partial(inverse_kernel, rows, chans, 1.0 / math.sqrt(pixels)),
        grid=(steps,),
        out_shape=jax.ShapeDtypeStruct((rows * chans, pixels), BF16),
        in_specs=[
            pl.BlockSpec((256 * chans, 128), lambda i: (0, 0)),
            pl.BlockSpec((512, pixels), lambda i: (0, 0)),
        ],
        out_specs=pl.BlockSpec((block, pixels), lambda i: (i, 0)),
        scratch_shapes=[
            pltpu.VMEM((256 * chans, 128), F32),
            pltpu.VMEM((4, rows * chans, 128), F32),
        ],
        compiler_params=pltpu.CompilerParams(vmem_limit_bytes=VMEM_LIMIT),
    )(field, table)
    return out.reshape(rows, chans, pixels)


def middle_kernel(
    rows,
    msg_ref,
    leg_hbm,
    kl_hbm,
    out_ref,
    leg,
    kl,
    got,
    spec,
    coef,
    filt,
    part,
    sib_part,
    transit,
    from_up,
    from_dn,
    reply,
    load_sem,
    own_sem,
    a2a_sem,
    ag_send,
    ag_recv,
    rs_send,
    rs_recv,
):
    modes, bands, cycles = leg.shape
    chans = 16
    span = modes // CHUNKS
    per = 2 * span
    b = lax.axis_index("blk")
    k = lax.axis_index("chan")
    y, core = lax.div(k, 2), lax.rem(k, 2)
    y_up, y_dn, y_far = lax.rem(y + 1, GY), lax.rem(y + GY - 1, GY), lax.rem(y + 2, GY)
    up, dn, far, sib = 2 * y_up + core, 2 * y_dn + core, 2 * y_far + core, 2 * y + 1 - core

    load_leg = pltpu.make_async_copy(leg_hbm, leg, load_sem.at[0])
    load_kl = pltpu.make_async_copy(kl_hbm, kl, load_sem.at[1])
    load_leg.start()
    load_kl.start()

    barrier = pltpu.get_barrier_semaphore()
    for other in (up, dn, sib):
        pl.semaphore_signal(barrier, inc=1, device_id={"chan": other}, device_id_type=MESH)

    def greet(j, _):
        pl.semaphore_signal(
            barrier, inc=1, device_id={"blk": lax.rem(b + j, NB)}, device_id_type=MESH
        )
        return 0

    lax.fori_loop(1, NB, greet, 0)
    pl.semaphore_wait(barrier, NB + 2)

    def sel(i):
        return pl.ds(span * i, span)

    def exchange(src, dst, which, i):
        def send(j):
            to = lax.rem(b + j, NB)
            pltpu.make_async_remote_copy(
                src_ref=src.at[to, sel(i)],
                dst_ref=dst.at[b, sel(i)],
                send_sem=a2a_sem.at[which, 0, i],
                recv_sem=a2a_sem.at[which, 1, i],
                device_id={"blk": to},
                device_id_type=MESH,
            ).start()

        def pair(j, _):
            send(j)
            send(NB - j)
            return 0

        lax.fori_loop(1, NB // 2, pair, 0)
        send(NB // 2)
        pltpu.make_async_copy(src.at[b, sel(i)], dst.at[b, sel(i)], own_sem.at[which, i]).start()

    def exchanged(src, dst, which, i):
        return pltpu.make_async_remote_copy(
            src_ref=src.at[pl.ds(0, NB - 1), sel(i)],
            dst_ref=dst.at[pl.ds(0, NB - 1), sel(i)],
            send_sem=a2a_sem.at[which, 0, i],
            recv_sem=a2a_sem.at[which, 1, i],
            device_id={"chan": sib},
            device_id_type=MESH,
        )

    def own_copy(src, dst, which, i):
        return pltpu.make_async_copy(src.at[b, sel(i)], dst.at[b, sel(i)], own_sem.at[which, i])

    def copy(src, dst, send, recv, slot, i, to):
        return pltpu.make_async_remote_copy(
            src_ref=src,
            dst_ref=dst,
            send_sem=send.at[i, slot],
            recv_sem=recv.at[i, slot],
            device_id={"chan": to},
            device_id_type=MESH,
        )

    def shard(i, owner, parts=None):
        lanes = pl.ds(pl.multiple_of(chans * owner, chans), chans)
        if parts is None:
            return spec.at[sel(i), :, lanes, :]
        return spec.at[sel(i), pl.ds(parts, 1), lanes, :]

    def gather_copy(slot, i):
        src, to = (
            (shard(i, k), up),
            (shard(i, k), dn),
            (shard(i, k), sib),
            (shard(i, dn, 0), up),
            (shard(i, up, 1), dn),
            (shard(i, dn), sib),
            (shard(i, up), sib),
            (shard(i, far, 0), sib),
            (shard(i, far, 1), sib),
        )[slot]
        return copy(src, src, ag_send, ag_recv, slot, i, to)

    def scatter_copy(slot, i):
        src, dst, to = (
            (part.at[sel(i), 1 - core], sib_part.at[sel(i)], sib),
            (part.at[sel(i), core, 0, y_far], transit.at[0, sel(i)], up),
            (part.at[sel(i), core, 1, y_far], transit.at[1, sel(i)], dn),
            (part.at[sel(i), core, 1, y_up], from_dn.at[1, sel(i)], up),
            (part.at[sel(i), core, 0, y_dn], from_up.at[0, sel(i)], dn),
            (transit.at[0, sel(i)], from_dn.at[0, sel(i)], up),
            (transit.at[1, sel(i)], from_up.at[1, sel(i)], dn),
        )[slot]
        return copy(src, dst, rs_send, rs_recv, slot, i, to)

    for i in range(CHUNKS):
        exchange(msg_ref, got, 0, i)

    def assemble(i):
        exchanged(msg_ref, got, 0, i).wait_recv()
        own_copy(msg_ref, got, 0, i).wait()
        mine = pl.ds(pl.multiple_of(chans * k, chans), chans)
        for m in range(span * i, span * (i + 1)):
            for p in range(2):
                pieces = [got[s, m, :, 64 * p : 64 * p + rows] for s in range(NB)]
                spec[m, p, mine, :] = jnp.concatenate(pieces, axis=1)
        for slot in (0, 1, 2):
            gather_copy(slot, i).start()

    def pass_on(i):
        gather_copy(0, i).wait_recv()
        gather_copy(3, i).start()
        gather_copy(5, i).start()
        gather_copy(1, i).wait_recv()
        gather_copy(4, i).start()
        gather_copy(6, i).start()

    def pass_far(i):
        gather_copy(3, i).wait_recv()
        gather_copy(7, i).start()
        gather_copy(4, i).wait_recv()
        gather_copy(8, i).start()

    def legendre(i):
        for slot in (2, 5, 6, 7, 8):
            gather_copy(slot, i).wait_recv()
        if i == 0:
            load_leg.wait()
            load_kl.wait()
        degree = k * bands + lax.broadcasted_iota(jnp.int32, (bands, 128), 0)
        for n in range(span):
            m = span * i + n
            sums = dot(leg[m], spec[m].reshape(2 * 128, cycles), NT)
            for p in range(2):
                kept = jnp.where(degree >= b * modes + m, sums[:, 128 * p : 128 * (p + 1)], 0.0)
                coef[pl.ds(2 * n + p, bands, stride=per), :] = kept

        group = 16 // per
        row_group = lax.div(lax.broadcasted_iota(jnp.int32, (16, 128), 0), per)

        def channels(g, _):
            for u in range(4):
                at = pl.multiple_of(16 * (4 * g + u), 16)
                left = coef[pl.ds(at, 16), :].astype(BF16)
                table = kl[pl.ds(group * (4 * g + u), group)]
                mixed = dot(left, table.reshape(group * 128, 128), NT)
                picked = mixed[:, :128]
                for t in range(1, group):
                    picked = jnp.where(row_group == t, mixed[:, 128 * t : 128 * (t + 1)], picked)
                filt[pl.ds(at, 16), :] = picked
            return 0

        lax.fori_loop(0, bands // group // 4, channels, 0)
        for n in range(span):
            m = span * i + n
            sides = [filt[pl.ds(2 * n + p, bands, stride=per), :].astype(BF16) for p in range(2)]
            left = jnp.concatenate(sides, axis=1).T
            for at in range(0, cycles, 256):
                tile = dot(left, leg[m, :, at : at + 256], NN).astype(BF16)
                for p in range(2):
                    for o in range(8):
                        first = 128 * p + 16 * o
                        part[m, o % 2, p, o // 2, :, at : at + 256] = tile[first : first + 16]
        scatter_copy(0, i).start()

    def add_sibling(i):
        scatter_copy(0, i).wait_recv()

        def add(t, _):
            m, p = span * i + lax.div(t, 2), lax.rem(t, 2)
            total = part[m, core, p].astype(F32) + sib_part[m, p].astype(F32)
            part[m, core, p] = total.astype(BF16)
            return 0

        lax.fori_loop(0, per, add, 0)
        for slot in (1, 2, 3, 4):
            scatter_copy(slot, i).start()

    def add_transit(i):
        for way, nearer in ((0, y_up), (1, y_dn)):
            scatter_copy(1 + way, i).wait_recv()
            for m in range(span * i, span * (i + 1)):
                total = transit[way, m].astype(F32) + part[m, core, way, nearer].astype(F32)
                transit[way, m] = total.astype(BF16)
            scatter_copy(5 + way, i).start()

    def answer(i):
        for slot in (3, 4, 5, 6):
            scatter_copy(slot, i).wait_recv()
        zeros = jnp.zeros((16, 64 - rows), F32)
        for m in range(span * i, span * (i + 1)):
            both = [
                part[m, core, p, y].astype(F32)
                + from_up[p, m].astype(F32)
                + from_dn[p, m].astype(F32)
                for p in range(2)
            ]
            for s in range(NB):
                lanes = slice(rows * s, rows * (s + 1))
                line = jnp.concatenate([both[0][:, lanes], zeros, both[1][:, lanes], zeros], axis=1)
                reply[s, m] = line.astype(BF16)
        exchange(reply, out_ref, 1, i)

    stages = (assemble, pass_on, pass_far, legendre, add_sibling, add_transit, answer)
    for tick in range(CHUNKS + len(stages) - 1):
        for n in reversed(range(len(stages))):
            if 0 <= tick - n < CHUNKS:
                stages[n](tick - n)

    for i in range(CHUNKS):
        last = exchanged(reply, out_ref, 1, i)
        last.wait_recv()
        own_copy(reply, out_ref, 1, i).wait()
        exchanged(msg_ref, got, 0, i).wait_send()
        last.wait_send()
        for slot in range(9):
            gather_copy(slot, i).wait_send()
        for slot in range(7):
            scatter_copy(slot, i).wait_send()


def middle(messages, legendre, kl, rows):
    modes, bands, cycles = legendre.shape
    chans = messages.shape[2]
    per = 2 * modes // CHUNKS
    vmem = pl.BlockSpec(memory_space=pltpu.VMEM)
    hbm = pl.BlockSpec(memory_space=pl.ANY)
    dma = pltpu.SemaphoreType.DMA
    return pl.pallas_call(
        functools.partial(middle_kernel, rows),
        out_shape=jax.ShapeDtypeStruct(messages.shape, BF16),
        in_specs=[vmem, hbm, hbm],
        out_specs=vmem,
        scratch_shapes=[
            pltpu.VMEM(legendre.shape, BF16),
            pltpu.VMEM(kl.shape, BF16),
            pltpu.VMEM(messages.shape, BF16),
            pltpu.VMEM((modes, 2, 128, cycles), BF16),
            pltpu.VMEM((bands * per, 128), F32),
            pltpu.VMEM((bands * per, 128), F32),
            pltpu.VMEM((modes, 2, 2, GY, chans, cycles), BF16),
            pltpu.VMEM((modes, 2, GY, chans, cycles), BF16),
            pltpu.VMEM((2, modes, chans, cycles), BF16),
            pltpu.VMEM((2, modes, chans, cycles), BF16),
            pltpu.VMEM((2, modes, chans, cycles), BF16),
            pltpu.VMEM(messages.shape, BF16),
            dma((2,)),
            dma((2, CHUNKS)),
            dma((2, 2, CHUNKS)),
            dma((CHUNKS, 9)),
            dma((CHUNKS, 9)),
            dma((CHUNKS, 7)),
            dma((CHUNKS, 7)),
        ],
        compiler_params=pltpu.CompilerParams(
            collective_id=0, has_side_effects=True, vmem_limit_bytes=VMEM_LIMIT
        ),
        cost_estimate=pl.CostEstimate(
            flops=6 * 10**9, bytes_accessed=14 * 10**6, transcendentals=0
        ),
    )(messages, legendre, kl)


def shards(sky_map, cycle_weight, legendre, kl_filter):
    rows, chans, pixels = sky_map.shape
    modes = legendre.shape[0]
    table = fourier_table(pixels, modes * NB)
    messages = forward(sky_map, cycle_weight, jnp.asarray(table))
    field = middle(messages.reshape(NB, modes, chans, 128), legendre, kl_filter, rows)
    return inverse(field.reshape(NB * modes * chans, 128), jnp.asarray(table.T.copy()), rows, chans)


def solution(mesh):
    in_specs = (P("blk", "chan", None), P("blk"), P("blk", "chan", None), P("chan", None, None))
    out_specs = P("blk", "chan", None)
    return jax.shard_map(shards, mesh=mesh, in_specs=in_specs, out_specs=out_specs, check_vma=False)
```

time: 315 us -> 112 us (0.36)
  Pallas kernels: 0 us -> 112 us
  waiting for transfers between devices: 94.5 us -> 0 us
  local copies, waits for them, and re-layouts: 91.8 us -> 0 us
  blocking collectives: 72.1 us -> 0 us
  matrix products: 30 us -> 0 us
  between operations: 13.5 us -> 0.01 us
  other arithmetic: 10.3 us -> 0 us
    pallas_call x0 -> x3, Pallas kernels: none -> 112 us  [the longest x1 97.7 us: middle(): pl.pallas_call(functools.partial(middle_kernel, rows), out_shape=jax.Shap...]
    all_to_all x2 -> x0, blocking collectives: 72.1 us -> none  [the longest x1 36.9 us: shards(): lax.all_to_all(spectra, 'blk', split_axis=3, concat_axis=0, tiled=True)]
    reduce_scatter x1 -> x0, waiting for transfers between devices: 50.3 us -> none  [shards(): lax.psum_scatter(jnp.einsum('mlr,mlpc->crpm', masked, filtered, preferred...]
    all_gather x1 -> x0, waiting for transfers between devices: 44.1 us -> none  [shards(): lax.all_gather(cycle_spectra, 'chan', axis=1, tiled=True)]
    unnamed x12 -> x0, local copies, waits for them, and re-layouts: 37.6 us -> none
    dot_general x5 -> x0, matrix products: 30 us -> none  [the longest x1 7.7 us: shards(): jnp.einsum('mlr,mlpc->crpm', masked, filtered, preferred_element_type=jnp...]
    all_to_all x3 -> x0, local copies, waits for them, and re-layouts: 27.5 us -> none  [the longest x1 20.1 us: shards(): lax.all_to_all(synth_field, 'blk', split_axis=1, concat_axis=3, tiled=True)]
    reduce_scatter x1 -> x0, local copies, waits for them, and re-layouts: 15.2 us -> none  [shards(): lax.psum_scatter(jnp.einsum('mlr,mlpc->crpm', masked, filtered, preferred...]
  transfers between devices with their start and end apart: 2 -> 0, of which waited for: 2 -> 0; matrix products, arithmetic and copies ran while one was open for 0% -> 0% of each run, Pallas kernels for 0% -> 0%
where the time goes in v1:
time: 112 us
  Pallas kernels  112 us (100%)
    pallas_call x1, Pallas kernels, middle(): pl.pallas_call(functools.partial(middle_kernel, rows), out_shape=jax.Shap...  97.7 us
    pallas_call x1, Pallas kernels, inverse(): pl.pallas_call(functools.partial(inverse_kernel, rows, chans, 1.0 / math....  7.2 us
    pallas_call x1, Pallas kernels, forward(): pl.pallas_call(functools.partial(forward_kernel, rows, chans, 1.0 / math....  6.85 us

profile of v1, /device:TPU:32, one launch (start us, length us, event | category | flops | bytes accessed | tf_op | source)
XLA Modules:
  0.0 111.7 jit_solution(8522511577295142222)
XLA Ops:
  0.0 6.9 %shard_map.64 = bf16[4096,128]{1,0:T(8,128)(2,1)} custom-call(bf16[896,2048]{1,0:T(8,128)(2,1)} %bitcast.5, f32[1,56]{1,0:T(1,128)} %bitcast.8, bf16[2048,512]{1,0:T(8,128)(2,1)} %constant.4.clone.table_ref), custom_call_target="tpu_custom_call" | custom-call | tf_op jit(solution)/shard_map/pallas_call | solution.py:66
  6.9 97.7 %shard_map.65 = bf16[32,8,16,128]{3,2,1,0:T(8,128)(2,1)} custom-call(bf16[32,8,16,128]{3,2,1,0:T(8,128)(2,1)} %bitcast.7, bf16[8,192,1792]{2,1,0:T(8,128)(2,1)} %leg_hbm.1, bf16[192,128,128]{2,1,0:T(8,128)(2,1)} %kl_hbm.1), custom_call_target="tpu_custom_call" | custom-call | flops 6000000000 | bytes 14000000 | tf_op jit(solution)/shard_map/pallas_call | solution.py:394
  104.5 7.2 %shard_map.66 = bf16[896,2048]{1,0:T(8,128)(2,1)} custom-call(bf16[4096,128]{1,0:T(8,128)(2,1)} %bitcast.6, bf16[512,2048]{1,0:T(8,128)(2,1)} %constant.5.clone.table_ref), custom_call_target="tpu_custom_call" | custom-call | tf_op jit(solution)/shard_map/pallas_call | solution.py:110

commit v2 on v0

v2 whole, which is shorter than its diff:
```python
import functools
import math

import jax
import jax.numpy as jnp
import numpy as np
from jax import lax
from jax.experimental import pallas as pl
from jax.experimental.pallas import tpu as pltpu
from jax.sharding import PartitionSpec as P

F32, BF16 = jnp.float32, jnp.bfloat16
MESH = pl.DeviceIdType.MESH
NT = (((1,), (1,)), ((), ()))
NN = (((1,), (0,)), ((), ()))
VMEM_LIMIT = 60 * 2**20
GX, GZ, GY = 4, 8, 4
NB = GX * GZ
MODES, GROUP = 8, 2
UNROLL = 4
AHEAD = 4
SCATTER, WINDOW, LAG = 3, 1, 2


def fourier_table(pixel_count, mode_count):
    phase = np.arange(pixel_count)[:, None] * np.arange(mode_count)[None, :] % pixel_count
    angles = phase.astype(np.float32) * np.float32(2.0 * math.pi / pixel_count)
    both = np.stack([np.cos(angles), -np.sin(angles)], axis=1).astype(jnp.bfloat16)
    both = both.reshape(pixel_count, 2, NB, 2, MODES // 2)
    return both.transpose(0, 3, 1, 4, 2).reshape(pixel_count, 2 * mode_count)


def identity(size):
    rows = lax.broadcasted_iota(jnp.int32, (size, size), 0)
    cols = lax.broadcasted_iota(jnp.int32, (size, size), 1)
    return jnp.where(rows == cols, 1.0, 0.0)


def dot(a, b, dims):
    return lax.dot_general(a, b, dims, preferred_element_type=F32)


def plan():
    steps = [("transform", 0), ("transform", 1), ("assemble", 0), ("assemble", 1), ("pass_on", 0)]
    for t in range(MODES + SCATTER + 4):
        steps += [("assemble", t + 2), ("pass_on", t + 1), ("pass_far", t)]
        r = t - SCATTER
        steps += [("add_transit", r - 1)]
        steps += [("add_sibling", i) for i in range(WINDOW - 1) if r == 0]
        steps += [("add_sibling", r + WINDOW - 1 if r >= 0 else -1), ("answer", r - LAG)]
        if t % 2:
            steps += [("analyse", (t - 1) // 2)]
        else:
            steps += [("synthesise", (t - 2) // 2)]
    steps += [("finish", 0), ("finish", 1)]
    count = {"transform": 2, "finish": 2, "analyse": MODES // GROUP, "synthesise": MODES // GROUP}
    return [(name, i) for name, i in steps if 0 <= i < count.get(name, MODES)]


def main_kernel(
    sky_hbm,
    weight_ref,
    table_hbm,
    leg_hbm,
    kl_hbm,
    out_ref,
    sky,
    table,
    leg,
    kl,
    wave,
    wide,
    msg,
    got,
    spec,
    coef,
    filt,
    part,
    sib_part,
    transit,
    from_up,
    from_dn,
    reply,
    back,
    load_sem,
    own_sem,
    a2a_sem,
    ag_send,
    ag_recv,
    rs_send,
    rs_recv,
):
    modes, bands, cycles = leg.shape
    chans, pixels = 16, sky.shape[1]
    rows = sky.shape[0] // chans
    half = modes // 2
    per = 2 * GROUP
    b = lax.axis_index("blk")
    k = lax.axis_index("chan")
    y, core = lax.div(k, 2), lax.rem(k, 2)
    y_up, y_dn, y_far = lax.rem(y + 1, GY), lax.rem(y + GY - 1, GY), lax.rem(y + 2, GY)
    up, dn, far, sib = 2 * y_up + core, 2 * y_dn + core, 2 * y_far + core, 2 * y + 1 - core

    load_sky = pltpu.make_async_copy(sky_hbm, sky, load_sem.at[0])
    load_table = pltpu.make_async_copy(table_hbm, table, load_sem.at[1])
    load_leg = pltpu.make_async_copy(leg_hbm, leg, load_sem.at[2])
    load_kl = pltpu.make_async_copy(kl_hbm, kl, load_sem.at[3])
    load_sky.start()
    load_table.start()

    barrier = pltpu.get_barrier_semaphore()
    for other in (up, dn, sib):
        pl.semaphore_signal(barrier, inc=1, device_id={"chan": other}, device_id_type=MESH)

    def greet(j, _):
        pl.semaphore_signal(
            barrier, inc=1, device_id={"blk": lax.rem(b + j, NB)}, device_id_type=MESH
        )
        return 0

    lax.fori_loop(1, NB, greet, 0)

    def own_copy(src, dst, which, i):
        return pltpu.make_async_copy(src.at[i, b], dst.at[i, b], own_sem.at[which, i])

    def exchange(src, dst, which, i):
        def send(j):
            to = lax.rem(b + j, NB)
            pltpu.make_async_remote_copy(
                src_ref=src.at[i, to],
                dst_ref=dst.at[i, b],
                send_sem=a2a_sem.at[which, 0, i],
                recv_sem=a2a_sem.at[which, 1, i],
                device_id={"blk": to},
                device_id_type=MESH,
            ).start()

        def pair(j, _):
            send(j)
            send(NB - j)
            return 0

        lax.fori_loop(1, NB // 2, pair, 0)
        send(NB // 2)
        own_copy(src, dst, which, i).start()

    def exchanged(src, dst, which, i):
        return pltpu.make_async_remote_copy(
            src_ref=src.at[i, pl.ds(0, NB - 1)],
            dst_ref=dst.at[i, pl.ds(0, NB - 1)],
            send_sem=a2a_sem.at[which, 0, i],
            recv_sem=a2a_sem.at[which, 1, i],
            device_id={"chan": sib},
            device_id_type=MESH,
        )

    def copy(src, dst, send, recv, slot, i, to):
        return pltpu.make_async_remote_copy(
            src_ref=src,
            dst_ref=dst,
            send_sem=send.at[i, slot],
            recv_sem=recv.at[i, slot],
            device_id={"chan": to},
            device_id_type=MESH,
        )

    def shard(i, owner, p=None):
        at = pl.ds(pl.multiple_of(chans * owner, chans), chans)
        return spec.at[i, :, at, :] if p is None else spec.at[i, p, at, :]

    def gather_copy(slot, i):
        src, to = (
            (shard(i, k), up),
            (shard(i, k), dn),
            (shard(i, k), sib),
            (shard(i, dn, 0), up),
            (shard(i, up, 1), dn),
            (shard(i, dn), sib),
            (shard(i, up), sib),
            (shard(i, far, 0), sib),
            (shard(i, far, 1), sib),
        )[slot]
        return copy(src, src, ag_send, ag_recv, slot, i, to)

    def scatter_copy(slot, i):
        src, dst, to = (
            (part.at[i, 1 - core], sib_part.at[i], sib),
            (part.at[i, core, 0, y_far], transit.at[0, i], up),
            (part.at[i, core, 1, y_far], transit.at[1, i], dn),
            (part.at[i, core, 1, y_up], from_dn.at[1, i], up),
            (part.at[i, core, 0, y_dn], from_up.at[0, i], dn),
            (transit.at[0, i], from_dn.at[0, i], up),
            (transit.at[1, i], from_up.at[1, i], dn),
        )[slot]
        return copy(src, dst, rs_send, rs_recv, slot, i, to)

    def transform(h):
        if h == 0:
            load_sky.wait()
            load_table.wait()
            load_leg.start()
            load_kl.start()
        weight = jnp.sum(identity(rows) * weight_ref[...], axis=1, keepdims=True)
        weight = weight * (1.0 / math.sqrt(pixels))
        eye = identity(128).astype(BF16)
        pad = jnp.zeros((64 - rows, 128), F32)
        found = dot(sky[...], table[:, 256 * h : 256 * (h + 1)], NN)
        for p in range(2):
            wave[p] = found[:, 128 * p : 128 * (p + 1)]
        for c in range(chans):
            real, imag = (wave[p, pl.ds(c, rows, stride=chans), :] * weight for p in range(2))
            both = jnp.concatenate([real, pad, imag, pad], axis=0).astype(BF16)
            wide[pl.ds(c, 128, stride=chans), :] = dot(eye, both, NT)
        for i in range(half):
            turned = wide[NB * chans * i : NB * chans * (i + 1), :].astype(BF16)
            msg[half * h + i] = turned.reshape(NB, chans, 128)
        if h == 0:
            pl.semaphore_wait(barrier, NB + 2)
            for i in range(AHEAD):
                exchange(msg, got, 0, i)

    def assemble(i):
        exchanged(msg, got, 0, i).wait_recv()
        own_copy(msg, got, 0, i).wait()
        if i + AHEAD < modes:
            exchange(msg, got, 0, i + AHEAD)
        mine = pl.ds(pl.multiple_of(chans * k, chans), chans)
        for p in range(2):
            pieces = [got[i, s, :, 64 * p : 64 * p + rows] for s in range(NB)]
            spec[i, p, mine, :] = jnp.concatenate(pieces, axis=1)
        for slot in range(3):
            gather_copy(slot, i).start()

    def pass_on(i):
        for n in range(2):
            gather_copy(n, i).wait_recv()
            gather_copy(3 + n, i).start()
            gather_copy(5 + n, i).start()

    def pass_far(i):
        for n in range(2):
            gather_copy(3 + n, i).wait_recv()
            gather_copy(7 + n, i).start()

    each = 16 // per
    rounds = bands // each // UNROLL

    def channels(g, _):
        row_group = lax.div(lax.broadcasted_iota(jnp.int32, (16, 128), 0), per)
        for u in range(UNROLL):
            at = pl.multiple_of(16 * (UNROLL * g + u), 16)
            left = coef[pl.ds(at, 16), :].astype(BF16)
            square = kl[pl.ds(each * (UNROLL * g + u), each)]
            mixed = dot(left, square.reshape(each * 128, 128), NT)
            picked = mixed[:, :128]
            for t in range(1, each):
                picked = jnp.where(row_group == t, mixed[:, 128 * t : 128 * (t + 1)], picked)
            filt[pl.ds(at, 16), :] = picked
        return 0

    def analyse(g):
        if g == 0:
            load_leg.wait()
            load_kl.wait()
        degree = k * bands + lax.broadcasted_iota(jnp.int32, (bands, 128), 0)
        for n in range(GROUP):
            i = GROUP * g + n
            for slot in (2, 5, 6, 7, 8):
                gather_copy(slot, i).wait_recv()
            sums = dot(leg[i], spec[i].reshape(2 * 128, cycles), NT)
            for p in range(2):
                kept = jnp.where(degree >= b * modes + i, sums[:, 128 * p : 128 * (p + 1)], 0.0)
                coef[pl.ds(2 * n + p, bands, stride=per), :] = kept
        lax.fori_loop(0, rounds // 2, channels, 0)

    def synthesise(g):
        lax.fori_loop(rounds // 2, rounds, channels, 0)
        for n in range(GROUP):
            i = GROUP * g + n
            sides = [filt[pl.ds(2 * n + p, bands, stride=per), :].astype(BF16) for p in range(2)]
            left = jnp.concatenate(sides, axis=1).T
            for at in range(0, cycles, 256):
                tile = dot(left, leg[i, :, at : at + 256], NN).astype(BF16)
                for p in range(2):
                    for o in range(8):
                        first = 128 * p + 16 * o
                        part[i, o % 2, p, o // 2, :, at : at + 256] = tile[first : first + 16]
            scatter_copy(0, i).start()

    def add_sibling(i):
        scatter_copy(0, i).wait_recv()

        def add(p, _):
            total = part[i, core, p].astype(F32) + sib_part[i, p].astype(F32)
            part[i, core, p] = total.astype(BF16)
            return 0

        lax.fori_loop(0, 2, add, 0)
        for slot in (1, 2, 3, 4):
            scatter_copy(slot, i).start()

    def add_transit(i):
        for n, nearer in ((0, y_up), (1, y_dn)):
            scatter_copy(1 + n, i).wait_recv()
            total = transit[n, i].astype(F32) + part[i, core, n, nearer].astype(F32)
            transit[n, i] = total.astype(BF16)
            scatter_copy(5 + n, i).start()

    def answer(i):
        for slot in (3, 4, 5, 6):
            scatter_copy(slot, i).wait_recv()
        zeros = jnp.zeros((16, 64 - rows), F32)
        both = [
            part[i, core, p, y].astype(F32)
            + from_up[p, i].astype(F32)
            + from_dn[p, i].astype(F32)
            for p in range(2)
        ]
        for s in range(NB):
            lanes = slice(rows * s, rows * (s + 1))
            line = jnp.concatenate([both[0][:, lanes], zeros, both[1][:, lanes], zeros], axis=1)
            reply[i, s] = line.astype(BF16)
        exchange(reply, back, 1, i)

    def finish(h):
        eye = identity(128).astype(BF16)
        for i in range(half):
            exchanged(reply, back, 1, half * h + i).wait_recv()
            own_copy(reply, back, 1, half * h + i).wait()
            turned = back[half * h + i].reshape(NB * chans, 128)
            wide[NB * chans * i : NB * chans * (i + 1), :] = turned.astype(F32)
        for c in range(chans):
            here = wide[pl.ds(c, 128, stride=chans), :].astype(BF16)
            turned = dot(eye, here, NT)
            for p in range(2):
                wave[p, pl.ds(c, rows, stride=chans), :] = turned[64 * p : 64 * p + rows]
        for p in range(2):
            at = 256 * h + 128 * p
            out_ref[:, at : at + 128] = wave[p].astype(BF16)

    stages = {
        f.__name__: f
        for f in (
            transform,
            assemble,
            pass_on,
            pass_far,
            analyse,
            synthesise,
            add_sibling,
            add_transit,
            answer,
            finish,
        )
    }
    for name, i in plan():
        stages[name](i)

    for i in range(modes):
        exchanged(msg, got, 0, i).wait_send()
        exchanged(reply, back, 1, i).wait_send()
        for slot in range(9):
            gather_copy(slot, i).wait_send()
        for slot in range(7):
            scatter_copy(slot, i).wait_send()


def main_call(sky, weight, table, legendre, kl):
    modes, bands, cycles = legendre.shape
    chans, (lines, pixels) = 16, sky.shape
    per = 2 * GROUP
    vmem = pl.BlockSpec(memory_space=pltpu.VMEM)
    hbm = pl.BlockSpec(memory_space=pl.ANY)
    dma = pltpu.SemaphoreType.DMA
    messages = pltpu.VMEM((modes, NB, chans, 128), BF16)
    return pl.pallas_call(
        main_kernel,
        out_shape=jax.ShapeDtypeStruct((lines, 512), BF16),
        in_specs=[hbm, vmem, hbm, hbm, hbm],
        out_specs=vmem,
        scratch_shapes=[
            pltpu.VMEM(sky.shape, BF16),
            pltpu.VMEM(table.shape, BF16),
            pltpu.VMEM(legendre.shape, BF16),
            pltpu.VMEM(kl.shape, BF16),
            pltpu.VMEM((2, lines, 128), F32),
            pltpu.VMEM((modes // 2 * NB * chans, 128), F32),
            messages,
            messages,
            pltpu.VMEM((modes, 2, 128, cycles), BF16),
            pltpu.VMEM((bands * per, 128), F32),
            pltpu.VMEM((bands * per, 128), F32),
            pltpu.VMEM((modes, 2, 2, GY, chans, cycles), BF16),
            pltpu.VMEM((modes, 2, GY, chans, cycles), BF16),
            pltpu.VMEM((2, modes, chans, cycles), BF16),
            pltpu.VMEM((2, modes, chans, cycles), BF16),
            pltpu.VMEM((2, modes, chans, cycles), BF16),
            messages,
            messages,
            dma((4,)),
            dma((2, modes)),
            dma((2, 2, modes)),
            dma((modes, 9)),
            dma((modes, 9)),
            dma((modes, 7)),
            dma((modes, 7)),
        ],
        compiler_params=pltpu.CompilerParams(
            collective_id=0, has_side_effects=True, vmem_limit_bytes=VMEM_LIMIT
        ),
        cost_estimate=pl.CostEstimate(
            flops=8 * 10**9, bytes_accessed=18 * 10**6, transcendentals=0
        ),
    )(sky, weight, table, legendre, kl)


def inverse_kernel(scale, field_ref, table_ref, out_ref):
    out_ref[...] = (dot(field_ref[...], table_ref[...], NN) * scale).astype(BF16)


def inverse(field, table):
    lines, pixels = field.shape[0], table.shape[1]
    block = 512
    return pl.pallas_call(
        functools.partial(inverse_kernel, 1.0 / math.sqrt(pixels)),
        grid=(pixels // block,),
        out_shape=jax.ShapeDtypeStruct((lines, pixels), BF16),
        in_specs=[
            pl.BlockSpec(field.shape, lambda i: (0, 0)),
            pl.BlockSpec((512, block), lambda i: (0, i)),
        ],
        out_specs=pl.BlockSpec((lines, block), lambda i: (0, i)),
        compiler_params=pltpu.CompilerParams(vmem_limit_bytes=VMEM_LIMIT),
    )(field, table)


def shards(sky_map, cycle_weight, legendre, kl_filter):
    rows, chans, pixels = sky_map.shape
    table = fourier_table(pixels, legendre.shape[0] * NB)
    sky = sky_map.reshape(rows * chans, pixels)
    weight = cycle_weight.reshape(1, rows)
    field = main_call(sky, weight, jnp.asarray(table), legendre, kl_filter)
    return inverse(field, jnp.asarray(table.T.copy())).reshape(rows, chans, pixels)


def solution(mesh):
    in_specs = (P("blk", "chan", None), P("blk"), P("blk", "chan", None), P("chan", None, None))
    out_specs = P("blk", "chan", None)
    return jax.shard_map(shards, mesh=mesh, in_specs=in_specs, out_specs=out_specs, check_vma=False)
```

time: 315 us -> 107 us (0.34)
  Pallas kernels: 0 us -> 106 us
  waiting for transfers between devices: 94.5 us -> 0 us
  local copies, waits for them, and re-layouts: 91.8 us -> 0 us
  blocking collectives: 72.1 us -> 0 us
  matrix products: 30 us -> 0 us
  between operations: 13.5 us -> 0.01 us
  other arithmetic: 10.3 us -> 0 us
    pallas_call x0 -> x2, Pallas kernels: none -> 106 us  [the longest x1 100 us: main_call(): pl.pallas_call(main_kernel, out_shape=jax.ShapeDtypeStruct((lines, 512),...]
    all_to_all x2 -> x0, blocking collectives: 72.1 us -> none  [the longest x1 36.9 us: shards(): lax.all_to_all(spectra, 'blk', split_axis=3, concat_axis=0, tiled=True)]
    reduce_scatter x1 -> x0, waiting for transfers between devices: 50.3 us -> none  [shards(): lax.psum_scatter(jnp.einsum('mlr,mlpc->crpm', masked, filtered, preferred...]
    all_gather x1 -> x0, waiting for transfers between devices: 44.1 us -> none  [shards(): lax.all_gather(cycle_spectra, 'chan', axis=1, tiled=True)]
    unnamed x12 -> x0, local copies, waits for them, and re-layouts: 37.6 us -> none
    dot_general x5 -> x0, matrix products: 30 us -> none  [the longest x1 7.7 us: shards(): jnp.einsum('mlr,mlpc->crpm', masked, filtered, preferred_element_type=jnp...]
    all_to_all x3 -> x0, local copies, waits for them, and re-layouts: 27.5 us -> none  [the longest x1 20.1 us: shards(): lax.all_to_all(synth_field, 'blk', split_axis=1, concat_axis=3, tiled=True)]
    reduce_scatter x1 -> x0, local copies, waits for them, and re-layouts: 15.2 us -> none  [shards(): lax.psum_scatter(jnp.einsum('mlr,mlpc->crpm', masked, filtered, preferred...]
  transfers between devices with their start and end apart: 2 -> 0, of which waited for: 2 -> 0; matrix products, arithmetic and copies ran while one was open for 0% -> 0% of each run, Pallas kernels for 0% -> 0%
where the time goes in v2:
time: 107 us; the launch traced here: 106 us
  Pallas kernels  106 us (99%)
    pallas_call x1, Pallas kernels, main_call(): pl.pallas_call(main_kernel, out_shape=jax.ShapeDtypeStruct((lines, 512),...  100 us
    pallas_call x1, Pallas kernels, inverse(): pl.pallas_call(functools.partial(inverse_kernel, 1.0 / math.sqrt(pixels))...  5.64 us

profile of v2, /device:TPU:32, one launch (start us, length us, event | category | flops | bytes accessed | tf_op | source)
XLA Modules:
  0.0 105.7 jit_solution(4921793881034591391)
XLA Ops:
  0.0 100.1 %shard_map.64.field_ref = bf16[896,512]{1,0:T(8,128)(2,1)} custom-call(bf16[896,2048]{1,0:T(8,128)(2,1)} %bitcast.3, f32[1,56]{1,0:T(1,128)} %bitcast.4, bf16[2048,512]{1,0:T(8,128)(2,1)} %constant.4.clone.table_hbm, bf16[8,192,1792]{2,1,0:T(8,128)(2,1)} %leg_hbm.1, bf16[192,128,128]{2,1,0:T(8,128)(2,1)} %kl_hbm.1), custom_call_target="tpu_custom_call" | custom-call | flops 8000000000 | bytes 18000000 | tf_op jit(solution)/shard_map/pallas_call | solution.py:376
  100.1 5.6 %shard_map.65 = bf16[896,2048]{1,0:T(8,128)(2,1)} custom-call(bf16[896,512]{1,0:T(8,128)(2,1)} %shard_map.64.field_ref, bf16[512,2048]{1,0:T(8,128)(2,1)} %constant.5.clone.table_ref), custom_call_target="tpu_custom_call" | custom-call | tf_op jit(solution)/shard_map/pallas_call | solution.py:424

commit v3 on v2

--- a/solution.py
+++ b/solution.py
@@ -17,9 +17,12 @@
 GX, GZ, GY = 4, 8, 4
 NB = GX * GZ
 MODES, GROUP = 8, 2
-UNROLL = 4
-AHEAD = 4
+UNROLL = 12
+BLOCK = 1024
+AHEAD = 3
 SCATTER, WINDOW, LAG = 3, 1, 2
+ORDER = (0, 1, 2, 4, 5, 6, 7, 3)
+EARLY = ORDER[-1]
 
 
 def fourier_table(pixel_count, mode_count):
@@ -41,19 +44,24 @@
 
 
 def plan():
-    steps = [("transform", 0), ("transform", 1), ("assemble", 0), ("assemble", 1), ("pass_on", 0)]
+    steps = [("transform", 0), ("early_send", 0), ("transform", 1), ("early_pass", 0)]
+    steps += [("assemble", 0), ("assemble", 1), ("pass_on", 0)]
     for t in range(MODES + SCATTER + 4):
-        steps += [("assemble", t + 2), ("pass_on", t + 1), ("pass_far", t)]
+        steps += [("early_exchange", t - 3)]
+        steps += [("assemble", t + 2 if t + 2 < MODES - 1 else -1)]
+        steps += [("pass_on", t + 1), ("pass_far", t)]
         r = t - SCATTER
         steps += [("add_transit", r - 1)]
         steps += [("add_sibling", i) for i in range(WINDOW - 1) if r == 0]
         steps += [("add_sibling", r + WINDOW - 1 if r >= 0 else -1), ("answer", r - LAG)]
+        steps += [("assemble", MODES - 1 if t == MODES - 1 else -1)]
         if t % 2:
             steps += [("analyse", (t - 1) // 2)]
         else:
             steps += [("synthesise", (t - 2) // 2)]
-    steps += [("finish", 0), ("finish", 1)]
+    steps += [("finish", 1), ("finish", 0)]
     count = {"transform": 2, "finish": 2, "analyse": MODES // GROUP, "synthesise": MODES // GROUP}
+    count |= {"early_send": 1, "early_pass": 1, "early_exchange": 1}
     return [(name, i) for name, i in steps if 0 <= i < count.get(name, MODES)]
 
 
@@ -72,6 +80,8 @@
     wide,
     msg,
     got,
+    early,
+    late,
     spec,
     coef,
     filt,
@@ -121,14 +131,17 @@
     lax.fori_loop(1, NB, greet, 0)
 
     def own_copy(src, dst, which, i):
+        if which == 0 and i == EARLY:
+            return pltpu.make_async_copy(early.at[:, b], late.at[b], own_sem.at[which, i])
         return pltpu.make_async_copy(src.at[i, b], dst.at[i, b], own_sem.at[which, i])
 
     def exchange(src, dst, which, i):
         def send(j):
             to = lax.rem(b + j, NB)
+            first = which == 0 and i == EARLY
             pltpu.make_async_remote_copy(
-                src_ref=src.at[i, to],
-                dst_ref=dst.at[i, b],
+                src_ref=early.at[:, to] if first else src.at[i, to],
+                dst_ref=late.at[b] if first else dst.at[i, b],
                 send_sem=a2a_sem.at[which, 0, i],
                 recv_sem=a2a_sem.at[which, 1, i],
                 device_id={"blk": to},
@@ -145,9 +158,11 @@
         own_copy(src, dst, which, i).start()
 
     def exchanged(src, dst, which, i):
+        some = pl.ds(0, NB - 1)
+        first = which == 0 and i == EARLY
         return pltpu.make_async_remote_copy(
-            src_ref=src.at[i, pl.ds(0, NB - 1)],
-            dst_ref=dst.at[i, pl.ds(0, NB - 1)],
+            src_ref=late.at[some] if first else src.at[i, some],
+            dst_ref=late.at[some] if first else dst.at[i, some],
             send_sem=a2a_sem.at[which, 0, i],
             recv_sem=a2a_sem.at[which, 1, i],
             device_id={"chan": sib},
@@ -180,6 +195,14 @@
             (shard(i, far, 0), sib),
             (shard(i, far, 1), sib),
         )[slot]
+        if i == EARLY and slot in (0, 1, 3, 4):
+            src = (
+                early.at[y],
+                early.at[y],
+                None,
+                early.at[y_dn, pl.ds(0, NB // 2)],
+                early.at[y_up, pl.ds(NB // 2, NB // 2)],
+            )[slot]
         return copy(src, src, ag_send, ag_recv, slot, i, to)
 
     def scatter_copy(slot, i):
@@ -216,14 +239,44 @@
             msg[half * h + i] = turned.reshape(NB, chans, 128)
         if h == 0:
             pl.semaphore_wait(barrier, NB + 2)
-            for i in range(AHEAD):
-                exchange(msg, got, 0, i)
+            exchange(msg, got, 0, ORDER[0])
+        else:
+            for i in range(1, AHEAD):
+                exchange(msg, got, 0, ORDER[i])
+
+    def early_send(_):
+        early[y] = msg[EARLY]
+        for slot in (0, 1):
+            gather_copy(slot, EARLY).start()
+
+    def early_pass(_):
+        for slot in (0, 1):
+            gather_copy(slot, EARLY).wait_recv()
+            gather_copy(3 + slot, EARLY).start()
+
+    def early_exchange(_):
+        for slot in (3, 4):
+            gather_copy(slot, EARLY).wait_recv()
+        exchange(msg, got, 0, EARLY)
+
+    def assemble_early():
+        for owner in range(GY):
+            at = pl.ds(pl.multiple_of(chans * (2 * owner + core), chans), chans)
+            for p in range(2):
+                pieces = [late[s, owner, :, 64 * p : 64 * p + rows] for s in range(NB)]
+                spec[EARLY, p, at, :] = jnp.concatenate(pieces, axis=1)
+        for slot in (2, 5, 6, 7, 8):
+            gather_copy(slot, EARLY).start()
 
     def assemble(i):
         exchanged(msg, got, 0, i).wait_recv()
         own_copy(msg, got, 0, i).wait()
-        if i + AHEAD < modes:
-            exchange(msg, got, 0, i + AHEAD)
+        if i == EARLY:
+            assemble_early()
+            return
+        later = ORDER.index(i) + AHEAD
+        if later < modes - 1:
+            exchange(msg, got, 0, ORDER[later])
         mine = pl.ds(pl.multiple_of(chans * k, chans), chans)
         for p in range(2):
             pieces = [got[i, s, :, 64 * p : 64 * p + rows] for s in range(NB)]
@@ -232,12 +285,16 @@
             gather_copy(slot, i).start()
 
     def pass_on(i):
+        if i == EARLY:
+            return
         for n in range(2):
             gather_copy(n, i).wait_recv()
             gather_copy(3 + n, i).start()
             gather_copy(5 + n, i).start()
 
     def pass_far(i):
+        if i == EARLY:
+            return
         for n in range(2):
             gather_copy(3 + n, i).wait_recv()
             gather_copy(7 + n, i).start()
@@ -264,7 +321,7 @@
             load_kl.wait()
         degree = k * bands + lax.broadcasted_iota(jnp.int32, (bands, 128), 0)
         for n in range(GROUP):
-            i = GROUP * g + n
+            i = ORDER[GROUP * g + n]
             for slot in (2, 5, 6, 7, 8):
                 gather_copy(slot, i).wait_recv()
             sums = dot(leg[i], spec[i].reshape(2 * 128, cycles), NT)
@@ -276,7 +333,7 @@
     def synthesise(g):
         lax.fori_loop(rounds // 2, rounds, channels, 0)
         for n in range(GROUP):
-            i = GROUP * g + n
+            i = ORDER[GROUP * g + n]
             sides = [filt[pl.ds(2 * n + p, bands, stride=per), :].astype(BF16) for p in range(2)]
             left = jnp.concatenate(sides, axis=1).T
             for at in range(0, cycles, 256):
@@ -342,6 +399,9 @@
         f.__name__: f
         for f in (
             transform,
+            early_send,
+            early_pass,
+            early_exchange,
             assemble,
             pass_on,
             pass_far,
@@ -354,7 +414,8 @@
         )
     }
     for name, i in plan():
-        stages[name](i)
+        by_mode = name in ("assemble", "pass_on", "pass_far", "add_sibling", "add_transit", "answer")
+        stages[name](ORDER[i] if by_mode else i)
 
     for i in range(modes):
         exchanged(msg, got, 0, i).wait_send()
@@ -387,6 +448,8 @@
             pltpu.VMEM((modes // 2 * NB * chans, 128), F32),
             messages,
             messages,
+            pltpu.VMEM((GY, NB, chans, 128), BF16),
+            pltpu.VMEM((NB, GY, chans, 128), BF16),
             pltpu.VMEM((modes, 2, 128, cycles), BF16),
             pltpu.VMEM((bands * per, 128), F32),
             pltpu.VMEM((bands * per, 128), F32),
@@ -420,7 +483,7 @@
 
 def inverse(field, table):
     lines, pixels = field.shape[0], table.shape[1]
-    block = 512
+    block = BLOCK
     return pl.pallas_call(
         functools.partial(inverse_kernel, 1.0 / math.sqrt(pixels)),
         grid=(pixels // block,),

time: 107 us -> 104 us (0.972)
  Pallas kernels: 106 us -> 103 us
    pallas_call x1, Pallas kernels: 100 us -> 97.9 us  [main_call(): pl.pallas_call(main_kernel, out_shape=jax.ShapeDtypeStruct((lines, 512),...]
where the time goes in v3:
time: 104 us; the launch traced here: 103 us
  Pallas kernels  103 us (99%)
    pallas_call x1, Pallas kernels, main_call(): pl.pallas_call(main_kernel, out_shape=jax.ShapeDtypeStruct((lines, 512),...  97.9 us
    pallas_call x1, Pallas kernels, inverse(): pl.pallas_call(functools.partial(inverse_kernel, 1.0 / math.sqrt(pixels))...  4.99 us

profile of v3, /device:TPU:32, one launch (start us, length us, event | category | flops | bytes accessed | tf_op | source)
XLA Modules:
  0.0 102.9 jit_solution(1245116639198348655)
XLA Ops:
  0.0 97.9 %shard_map.64.field_ref = bf16[896,512]{1,0:T(8,128)(2,1)} custom-call(bf16[896,2048]{1,0:T(8,128)(2,1)} %bitcast.3, f32[1,56]{1,0:T(1,128)} %bitcast.4, bf16[2048,512]{1,0:T(8,128)(2,1)} %constant.4.clone.table_hbm, bf16[8,192,1792]{2,1,0:T(8,128)(2,1)} %leg_hbm.1, bf16[192,128,128]{2,1,0:T(8,128)(2,1)} %kl_hbm.1), custom_call_target="tpu_custom_call" | custom-call | flops 8000000000 | bytes 18000000 | tf_op jit(solution)/shard_map/pallas_call | solution.py:437
  97.9 5.0 %shard_map.65 = bf16[896,2048]{1,0:T(8,128)(2,1)} custom-call(bf16[896,512]{1,0:T(8,128)(2,1)} %shard_map.64.field_ref, bf16[512,2048]{1,0:T(8,128)(2,1)} %constant.5.clone.table_ref), custom_call_target="tpu_custom_call" | custom-call | tf_op jit(solution)/shard_map/pallas_call | solution.py:487

commit v4 on v3

--- a/solution.py
+++ b/solution.py
@@ -17,7 +17,7 @@
 GX, GZ, GY = 4, 8, 4
 NB = GX * GZ
 MODES, GROUP = 8, 2
-UNROLL = 12
+UNROLL = 24
 BLOCK = 1024
 AHEAD = 3
 SCATTER, WINDOW, LAG = 3, 1, 2

time: 104 us -> 103 us (level)
  no operation moved by 1% of the time
where the time goes in v4:
time: 103 us
  Pallas kernels  103 us (100%)
    pallas_call x1, Pallas kernels, main_call(): pl.pallas_call(main_kernel, out_shape=jax.ShapeDtypeStruct((lines, 512),...  97.7 us
    pallas_call x1, Pallas kernels, inverse(): pl.pallas_call(functools.partial(inverse_kernel, 1.0 / math.sqrt(pixels))...  5 us

profile of v4, /device:TPU:32, one launch (start us, length us, event | category | flops | bytes accessed | tf_op | source)
XLA Modules:
  0.0 102.7 jit_solution(14998014649539501162)
XLA Ops:
  0.0 97.7 %shard_map.64.field_ref = bf16[896,512]{1,0:T(8,128)(2,1)} custom-call(bf16[896,2048]{1,0:T(8,128)(2,1)} %bitcast.3, f32[1,56]{1,0:T(1,128)} %bitcast.4, bf16[2048,512]{1,0:T(8,128)(2,1)} %constant.4.clone.table_hbm, bf16[8,192,1792]{2,1,0:T(8,128)(2,1)} %leg_hbm.1, bf16[192,128,128]{2,1,0:T(8,128)(2,1)} %kl_hbm.1), custom_call_target="tpu_custom_call" | custom-call | flops 8000000000 | bytes 18000000 | tf_op jit(solution)/shard_map/pallas_call | solution.py:437
  97.7 5.0 %shard_map.65 = bf16[896,2048]{1,0:T(8,128)(2,1)} custom-call(bf16[896,512]{1,0:T(8,128)(2,1)} %shard_map.64.field_ref, bf16[512,2048]{1,0:T(8,128)(2,1)} %constant.5.clone.table_ref), custom_call_target="tpu_custom_call" | custom-call | tf_op jit(solution)/shard_map/pallas_call | solution.py:487
